TPU v7x, 512 devices: a whole 4x4x16 slice. The times are simulated.
512 devices in a mesh: view: 4 (over x), dev: 128 (over z, y, core).
Axes of the slice: x: 4, y: 4, z: 16, core: 2. Of those that a mesh axis runs over, the one named last changes fastest.
Arguments:
- attributes: float32 [59, 65536], P(None, 'dev'), may hold values from -6 to 8, as said below
- camera: float32 [4, 6], P('view'), may hold values from -0.2 to 0.2
- list_owner: int32 [4, 512, 256, 1], P('view', 'dev'), may hold values from 0 to 127; in each aligned block of 1024 rows (0 to 1023, 1024 to 2047, ..., all dimensions but the last counted through in order) at most 16 rows name the same one
- list_local: int32 [4, 512, 256], P('view', 'dev'), may hold values from 0 to 511
- term_depth: int32 [4, 512, 256], P('view', 'dev'), may hold values from 1 to 256
- image_cot: float32 [4, 3, 512, 256], P('view', None, 'dev'), may hold values from -6 to 6
Outputs:
- image: float32 [4, 3, 512, 256], P('view', None, 'dev')
- attr_grad: float32 [59, 65536], P(None, 'dev')
Inputs may be any that keep to these rules, and one draw needn't show every extreme that they name: `attributes`: the quaternion's real part lies in 0.5 to 1.5, the third position coordinate in 4 to 8. `list_owner`: among the slots of one device's tiles of one view no owner is named more than 16 times.
All inputs are finite; a program needn't handle non-finite values.
Results may differ from a plain program's by a relative error of at most 0.0003.
Values sent between devices are 32-bit elements; how exact they have to be, the bound alone decides.
No kernel may reach another device: no remote copies, remote signals or barrier semaphores. Data moves between devices by JAX's collectives and lax.ppermute only.
A program may use at most 64 MiB of HBM per device.

v0:
```python
import jax
import jax.numpy as jnp
from jax import lax
from jax.sharding import PartitionSpec as P

TILE_COLS = 16
SH_C0 = 0.28209479177387814
SH_C1 = 0.4886025119029199
SH_C2 = (
    1.0925484305920792,
    -1.0925484305920792,
    0.31539156525252005,
    -1.0925484305920792,
    0.5462742152960396,
)
SH_C3 = (
    -0.5900435899266435,
    2.890611442640554,
    -0.4570457994644658,
    0.3731763325901154,
    -0.4570457994644658,
    1.445305721320277,
    -0.5900435899266435,
)
BLUR = 1e-05


def rotation(angles):
    one = jnp.ones((), jnp.float32)
    zero = jnp.zeros((), jnp.float32)
    cosx, sinx = (jnp.cos(angles[0]), jnp.sin(angles[0]))
    cosy, siny = (jnp.cos(angles[1]), jnp.sin(angles[1]))
    cosz, sinz = (jnp.cos(angles[2]), jnp.sin(angles[2]))
    rot_x = jnp.stack(
        [
            jnp.stack([one, zero, zero]),
            jnp.stack([zero, cosx, -sinx]),
            jnp.stack([zero, sinx, cosx]),
        ]
    )
    rot_y = jnp.stack(
        [
            jnp.stack([cosy, zero, siny]),
            jnp.stack([zero, one, zero]),
            jnp.stack([-siny, zero, cosy]),
        ]
    )
    rot_z = jnp.stack(
        [
            jnp.stack([cosz, -sinz, zero]),
            jnp.stack([sinz, cosz, zero]),
            jnp.stack([zero, zero, one]),
        ]
    )
    high = lax.Precision.HIGHEST
    return jnp.dot(rot_z, jnp.dot(rot_y, rot_x, precision=high), precision=high)


def harmonics(dirx, diry, dirz):
    xx, yy, zz = (dirx * dirx, diry * diry, dirz * dirz)
    return [
        SH_C0 + 0.0 * dirx,
        -SH_C1 * diry,
        SH_C1 * dirz,
        -SH_C1 * dirx,
        SH_C2[0] * dirx * diry,
        SH_C2[1] * diry * dirz,
        SH_C2[2] * (2.0 * zz - xx - yy),
        SH_C2[3] * dirx * dirz,
        SH_C2[4] * (xx - yy),
        SH_C3[0] * diry * (3.0 * xx - yy),
        SH_C3[1] * dirx * diry * dirz,
        SH_C3[2] * diry * (4.0 * zz - xx - yy),
        SH_C3[3] * dirz * (2.0 * zz - 3.0 * xx - 3.0 * yy),
        SH_C3[4] * dirx * (4.0 * zz - xx - yy),
        SH_C3[5] * dirz * (xx - yy),
        SH_C3[6] * dirx * (xx - 3.0 * yy),
    ]


def project(attrs, cam):
    rot = rotation(cam[0:3])
    shift = cam[3:6]
    pos = attrs[0:3]
    campos = jnp.dot(rot, pos, precision=lax.Precision.HIGHEST) + shift[:, None]
    posx, posy, posz = (campos[0], campos[1], campos[2])
    inverse = 1.0 / posz
    jac = [
        [inverse, 0.0 * inverse, -posx * inverse * inverse],
        [0.0 * inverse, inverse, -posy * inverse * inverse],
    ]
    tmat = [[sum((jac[r][i] * rot[i, j] for i in range(3))) for j in range(3)] for r in range(2)]
    scale = jnp.exp(attrs[3:6])
    quat = attrs[6:10]
    quat = quat * lax.rsqrt(jnp.sum(quat * quat, axis=0))
    qw, qa, qb, qc = (quat[0], quat[1], quat[2], quat[3])
    rgau = [
        [1 - 2 * (qb * qb + qc * qc), 2 * (qa * qb - qw * qc), 2 * (qa * qc + qw * qb)],
        [2 * (qa * qb + qw * qc), 1 - 2 * (qa * qa + qc * qc), 2 * (qb * qc - qw * qa)],
        [2 * (qa * qc - qw * qb), 2 * (qb * qc + qw * qa), 1 - 2 * (qa * qa + qb * qb)],
    ]
    mscaled = [[rgau[i][k] * scale[k] for k in range(3)] for i in range(3)]
    cov = [
        [sum((mscaled[i][k] * mscaled[j][k] for k in range(3))) for j in range(3)] for i in range(3)
    ]
    sig = [
        [
            sum((tmat[r][i] * cov[i][j] * tmat[s][j] for i in range(3) for j in range(3)))
            for s in range(2)
        ]
        for r in range(2)
    ]
    sig_a = sig[0][0] + BLUR
    sig_b = sig[0][1]
    sig_c = sig[1][1] + BLUR
    det = sig_a * sig_c - sig_b * sig_b
    centre = [
        -(rot[0, j] * shift[0] + rot[1, j] * shift[1] + rot[2, j] * shift[2]) for j in range(3)
    ]
    dirs = [pos[j] - centre[j] for j in range(3)]
    norm_inv = lax.rsqrt(dirs[0] * dirs[0] + dirs[1] * dirs[1] + dirs[2] * dirs[2])
    basis = harmonics(dirs[0] * norm_inv, dirs[1] * norm_inv, dirs[2] * norm_inv)
    colors = [0.5 + sum((basis[k] * attrs[11 + 3 * k + ch] for k in range(16))) for ch in range(3)]
    opacity = jax.nn.sigmoid(attrs[10])
    return jnp.stack(
        [posx * inverse, posy * inverse, sig_c / det, -sig_b / det, sig_a / det, opacity] + colors
    )


def pixel_coords(tile, ntiles):
    pixel = jnp.arange(256, dtype=jnp.int32)
    col = tile % TILE_COLS
    row = tile // TILE_COLS
    xs = ((col * 16 + pixel % 16).astype(jnp.float32) + 0.5) / (16.0 * TILE_COLS) - 0.5
    ys = ((row * 16 + pixel // 16).astype(jnp.float32) + 0.5) / (16.0 * (ntiles // TILE_COLS)) - 0.5
    return (xs, ys)


def tile_color(rows, xs, ys, depth):
    slot_entries = rows.shape[1]
    delta_x = xs[:, None] - rows[0][None, :]
    delta_y = ys[:, None] - rows[1][None, :]
    power = (
        0.5 * (rows[2][None, :] * delta_x * delta_x + rows[4][None, :] * delta_y * delta_y)
        + rows[3][None, :] * delta_x * delta_y
    )
    live = (jnp.arange(slot_entries, dtype=jnp.int32)[None, :] < depth[:, None]).astype(jnp.float32)
    alpha = rows[5][None, :] * jnp.exp(-power) * live
    keep = jnp.cumprod(1.0 - alpha, axis=1)
    trans = jnp.concatenate([jnp.ones((xs.shape[0], 1), jnp.float32), keep[:, :-1]], axis=1)
    weight = trans * alpha
    return jnp.einsum("ps,cs->cp", weight, rows[6:9], precision=lax.Precision.HIGHEST)


def composite(rows_slot, first_tile, ntiles, depth, cotangent):
    tile_entries = depth.shape[0]
    rows_tiles = jnp.transpose(rows_slot.reshape(rows_slot.shape[0], tile_entries, -1), (1, 0, 2))

    def tile_work(packed):
        rows, tile, pixel_depth, pixel_cot = packed
        xs, ys = pixel_coords(tile, ntiles)
        color, pull = jax.vjp(lambda r: tile_color(r, xs, ys, pixel_depth), rows)
        return (color, pull(pixel_cot)[0])

    tile_ids = first_tile + jnp.arange(tile_entries, dtype=jnp.int32)
    color, grads = lax.map(tile_work, (rows_tiles, tile_ids, depth, cotangent))
    return (color, jnp.transpose(grads, (1, 0, 2)).reshape(rows_slot.shape[0], -1))


def per_device(attributes, camera, list_owner, list_local, term_depth, image_cot):
    device_total = lax.axis_size("dev")
    g_dev = attributes.shape[1]
    tile_entries = list_local.shape[1]
    slot_entries = list_local.shape[2]
    slot_total = tile_entries * slot_entries
    slot_capacity = 2 * slot_total // device_total
    ntiles = tile_entries * device_total
    owner = list_owner[0, :, :, 0].reshape(-1)
    local_ids = list_local[0].reshape(-1)
    onehot = (owner[:, None] == jnp.arange(device_total, dtype=jnp.int32)[None, :]).astype(
        jnp.int32
    )
    counts = jnp.sum(onehot, axis=0)
    starts = jnp.cumsum(counts) - counts
    initial_slot = jnp.sum(onehot * starts[None, :], axis=1)
    sorted_order = jnp.argsort(owner, stable=True)
    rank = (
        jnp.zeros((slot_total,), jnp.int32)
        .at[sorted_order]
        .set(jnp.arange(slot_total, dtype=jnp.int32) - initial_slot[sorted_order])
    )
    position = owner * slot_capacity + rank
    request = jnp.zeros((device_total * slot_capacity,), jnp.int32).at[position].set(local_ids)
    asked = lax.all_to_all(
        request.reshape(device_total, slot_capacity), "dev", split_axis=0, concat_axis=0, tiled=True
    ).reshape(-1)
    cam = camera[0]
    first_tile = lax.axis_index("dev") * tile_entries
    depth = term_depth[0]
    cotangent = jnp.transpose(image_cot[0], (1, 0, 2))
    total = None
    rows_owner, pull_owner = jax.vjp(lambda a: project(a, cam), attributes)
    sent = rows_owner[:, asked]
    arrived = lax.all_to_all(
        sent.reshape(9, device_total, slot_capacity), "dev", split_axis=1, concat_axis=1, tiled=True
    ).reshape(9, -1)
    rows_slot = arrived[:, position]
    color, grad_slot = composite(rows_slot, first_tile, ntiles, depth, cotangent)
    grad_buffer = (
        jnp.zeros((9, device_total * slot_capacity), jnp.float32).at[:, position].set(grad_slot)
    )
    returned = lax.all_to_all(
        grad_buffer.reshape(9, device_total, slot_capacity),
        "dev",
        split_axis=1,
        concat_axis=1,
        tiled=True,
    ).reshape(9, -1)
    grad_rows = jnp.zeros((9, g_dev), jnp.float32).at[:, asked].add(returned)
    attr_grad = pull_owner(grad_rows)[0]
    total = lax.psum(attr_grad, "view")
    image = jnp.transpose(color, (1, 0, 2))[None]
    return (image, total)


def solution(mesh):
    in_specs = (
        P(None, "dev"),
        P("view", None),
        P("view", "dev", None, None),
        P("view", "dev", None),
        P("view", "dev", None),
        P("view", None, "dev", None),
    )
    out_specs = (P("view", None, "dev", None), P(None, "dev"))
    return jax.shard_map(
        per_device, mesh=mesh, in_specs=in_specs, out_specs=out_specs, check_vma=False
    )
```

profile of v0, /device:TPU:8, one launch (start us, length us, event | category | flops | bytes accessed | tf_op | source)
XLA Modules:
  0.0 316.3 jit_solution(12072224999658758813)
XLA Ops:
  7.2 0.9 convert_reduce_fusion
  8.8 4.4 %sort.17 = (s32[1024]{0:T(1024)}, s32[1024]{0:T(1024)S(1)}) sort(s32[1024]{0:T(1024)S(1)} %bitcast.195, s32[1024]{0:T(1024)S(1)} %iota.41), dimensions={0}, to_apply=%region_1.0 | sort | flops 10240 | bytes 16384 | tf_op jit(solution)/shard_map/jit(argsort)/sort | solution.py:186
  13.9 4.5 %gather_fusion = s32[1024]{0:T(1024)S(1)} fusion(s32[1024]{0:T(1024)S(1)} %select_reduce_fusion, s32[1024]{0:T(1024)S(1)} %get-tuple-element.358), kind=kCustom, calls=%fused_computation | custom fusion | bytes 12288 | tf_op jit(solution)/shard_map/gather | solution.py:190
  18.5 4.3 %scatter_custom_fusion = s32[1024]{0:T(1024)S(1)} fusion(s32[1024]{0:T(1024)S(1)} %get-tuple-element.359, s32[1024]{0:T(1024)S(1)} %iota_subtract_fusion, s32[]{:T(128)} %constant.192.clone.1), kind=kCustom, calls=%fused_computation.292 | custom fusion | bytes 4100 | tf_op jit(solution)/shard_map/scatter | solution.py:190
  22.8 4.3 %scatter_custom_fusion.1 = s32[2048]{0:T(1024)S(1)} fusion(s32[1024]{0:T(1024)S(1)} %get-tuple-element.215, s32[1024]{0:T(1024)S(1)} %bitcast.202, s32[]{:T(128)} %constant.192.clone.1), kind=kCustom, calls=%fused_computation.165 | custom fusion | bytes 8196 | tf_op jit(solution)/shard_map/scatter | solution.py:193
  27.2 0.7 all_to_all.12
  27.9 19.5 %all-to-all-start = ((s32[128,1,16]{2,1,0:T(1,128)}), s32[128,1,16]{2,1,0:T(1,128)S(1)}, u32[]{:S(2)}, u32[]{:S(2)}) async-start(s32[128,1,16]{2,1,0:T(1,128)} %bitcast.48), calls=%async_computation | async-start | bytes 131072 | tf_op jit(solution)/shard_map/all_to_all | solution.py:194
  54.8 0.7 fusion.152
  74.5 2.1 fusion.143
  77.4 0.8 reduce.4
  78.4 5.5 %gather_fusion.1 = f32[2048,9]{1,0:T(8,128)S(1)} fusion(f32[9,512]{0,1:T(8,128)S(1)} %copy.57, s32[2048]{0:T(1024)S(1)} %broadcast_clamp_fusion), kind=kCustom, calls=%fused_computation.1 | custom fusion | bytes 155648 | tf_op jit(solution)/shard_map/gather | solution.py:203
  83.8 1.4 reshape.321
  85.3 16.2 %all-to-all-start.1 = ((f32[128,1,144]{2,1,0:T(1,128)}), f32[128,1,144]{2,1,0:T(1,128)S(1)}, u32[]{:S(2)}, u32[]{:S(2)}) async-start(f32[128,1,144]{2,1,0:T(1,128)} %reshape.321), calls=%async_computation.1 | async-start | bytes 262144 | tf_op jit(solution)/shard_map/all_to_all | solution.py:204
  101.8 15.8 %all-to-all-done.1 = f32[128,1,144]{2,1,0:T(1,128)S(1)} async-done(((f32[128,1,144]{2,1,0:T(1,128)}), f32[128,1,144]{2,1,0:T(1,128)S(1)}, u32[]{:S(2)}, u32[]{:S(2)}) %all-to-all-start.1) | async-done | bytes 73760 | tf_op jit(solution)/shard_map/all_to_all | solution.py:204
  118.2 0.9 reduce.5
  119.8 2.8 gather_fusion.2
  123.4 82.5 %while.15 = (s32[]{:T(128)}, f32[4,3,256]{2,0,1:T(4,128)S(1)}, f32[4,9,256]{2,1,0:T(8,128)S(1)}, f32[4,9,256]{2,1,0:T(8,128)S(1)}, s32[4,256]{1,0:T(4,128)}, /*i...) while((s32[]{:T(128)}, f32[4,3,256]{2,0,1:T(4,128)S(1)}, ...), condition=%wide.region_14.15_spmd, body=%wide.region_7.14_spmd.sunk | while | flops 15078685 | bytes 22935272 | solution.py:166
  126.6 0.7 constant_dynamic-slice_fusion.10
  133.4 0.7 slice-done.9
  147.2 0.7 constant_dynamic-slice_fusion.10
  167.9 0.7 constant_dynamic-slice_fusion.10
  188.5 0.7 constant_dynamic-slice_fusion.10
  206.8 3.3 %scatter_custom_fusion.2 = f32[9,2048]{0,1:T(8,128)S(1)} fusion(s32[1024]{0:T(1024)S(1)} %get-tuple-element.215, f32[1024,9]{1,0:T(8,128)S(1)} %copy.62, f32[]{:T(128)} %constant.193.clone.1), kind=kCustom, calls=%fused_computation.138 | custom fusion | bytes 73732 | tf_op jit(solution)/shard_map/scatter | solution.py:210
  210.1 0.8 reshape.323
  210.9 23.2 %all_to_all.19 = f32[128,1,144]{2,1,0:T(1,128)S(1)} all-to-all(f32[128,1,144]{2,1,0:T(1,128)S(1)} %reshape.323), channel_id=1, replica_groups=mesh['view'=4,'dev'=128] {'dev'}, dimensions={0} | all-to-all | bytes 147456 | tf_op jit(solution)/shard_map/all_to_all | solution.py:212
  234.0 0.9 reduce.6
  235.6 12.1 %scatter_custom_fusion.3 = f32[9,512]{0,1:T(8,128)S(1)} fusion(s32[2048]{0:T(1024)S(1)} %bitcast.199, f32[2048,9]{1,0:T(8,128)S(1)} %bitcast.148, f32[]{:T(128)} %constant.193.clone.1), kind=kCustom, calls=%fused_computation.144 | custom fusion | flops 18432 | bytes 18436 | tf_op jit(solution)/shard_map/scatter-add | solution.py:219
  250.3 5.8 %fusion.98 = (f32[1,512]{1,0:T(1,128)S(1)}, f32[1,512]{1,0:T(1,128)S(1)}, f32[1,512]{1,0:T(1,128)S(1)}, f32[1,512]{1,0:T(1,128)S(1)}, f32[1,512]{1,0:T(1,128)S(1...) fusion(f32[1,512]{1,0:T(1,128)S(1)} %copy.82, f32[1,512]{1,0:T(1,128)S(1)} %copy.81, ...), kind=kLoop, calls=%fused_computation.325 | loop fusion | flops 81920 | bytes 100388 | tf_op jit(solution)/shard_map/transpose(jvp())/neg | solution.py:87
  256.1 2.0 negate_add_fusion.1
  258.4 0.9 pad_add_fusion.9
  259.3 48.5 %all-reduce.135.cloned.1.call-done = f32[59,512]{1,0:T(8,128)} async-done(((f32[59,512]{1,0:T(8,128)}), f32[59,512]{1,0:T(8,128)}) %all-reduce.135.cloned.1.call-update) | async-done | bytes 120848 | tf_op jit(solution)/shard_map/psum | solution.py:221
  307.8 1.6 copy.180
  (873 shorter events, 77.2 us)
Async XLA Ops:
  7.2 0.9 copy-start.16
  8.1 0.7 copy-start.12
  18.5 28.9 %copy-start.11 = (f32[59,512]{1,0:T(8,128)S(1)}, f32[59,512]{1,0:T(8,128)}, u32[]{:S(2)}) copy-start(f32[59,512]{1,0:T(8,128)} %param.8) | copy-start | bytes 362500
  27.9 49.1 %all-to-all-start = ((s32[128,1,16]{2,1,0:T(1,128)}), s32[128,1,16]{2,1,0:T(1,128)S(1)}, u32[]{:S(2)}, u32[]{:S(2)}) async-start(s32[128,1,16]{2,1,0:T(1,128)} %bitcast.48), calls=%async_computation | async-start | bytes 131072 | tf_op jit(solution)/shard_map/all_to_all | solution.py:194
  85.3 16.5 %copy-start.15 = (f32[1,3,4,256]{3,2,1,0:T(4,128)S(1)}, f32[1,3,4,256]{3,2,1,0:T(4,128)}, u32[]{:S(2)}) copy-start(f32[1,3,4,256]{3,2,1,0:T(4,128)} %param.13) | copy-start | bytes 36868
  85.3 32.3 %all-to-all-start.1 = ((f32[128,1,144]{2,1,0:T(1,128)}), f32[128,1,144]{2,1,0:T(1,128)S(1)}, u32[]{:S(2)}, u32[]{:S(2)}) async-start(f32[128,1,144]{2,1,0:T(1,128)} %reshape.321), calls=%async_computation.1 | async-start | bytes 262144 | tf_op jit(solution)/shard_map/all_to_all | solution.py:204
  101.5 206.3 %all-reduce.135.cloned.1.call-start = ((), (), s32[]{:S(2)}) async-start(), calls=%async_computation.3 | async-start | bytes 262144 | tf_op jit(solution)/shard_map/psum | solution.py:221
  128.3 11.2 %copy-start = (f32[256,128]{0,1:T(8,128)}, f32[256,128]{0,1:T(8,128)S(1)}, u32[]{:S(2)}) copy-start(f32[256,128]{0,1:T(8,128)S(1)} %slice.1658) | copy-start | bytes 393220 | tf_op jit(solution)/shard_map/while
  132.4 5.5 %copy-start.2 = (f32[256,64]{0,1:T(8,128)}, f32[256,64]{0,1:T(8,128)S(1)}, u32[]{:S(2)}) copy-start(f32[256,64]{0,1:T(8,128)S(1)} %slice.1665) | copy-start | bytes 196612 | tf_op jit(solution)/shard_map/while
  132.5 4.0 %copy-start.4 = (f32[256,32]{0,1:T(8,128)}, f32[256,32]{0,1:T(8,128)S(1)}, u32[]{:S(2)}) copy-start(f32[256,32]{0,1:T(8,128)S(1)} %slice.1666) | copy-start | bytes 98308 | tf_op jit(solution)/shard_map/while
  132.6 2.4 copy-start.6
  132.7 1.6 copy-start.8
  133.4 0.7 slice-start.9
  138.0 0.7 slice-start.1
  148.9 11.2 %copy-start = (f32[256,128]{0,1:T(8,128)}, f32[256,128]{0,1:T(8,128)S(1)}, u32[]{:S(2)}) copy-start(f32[256,128]{0,1:T(8,128)S(1)} %slice.1658) | copy-start | bytes 393220 | tf_op jit(solution)/shard_map/while
  153.0 5.5 %copy-start.2 = (f32[256,64]{0,1:T(8,128)}, f32[256,64]{0,1:T(8,128)S(1)}, u32[]{:S(2)}) copy-start(f32[256,64]{0,1:T(8,128)S(1)} %slice.1665) | copy-start | bytes 196612 | tf_op jit(solution)/shard_map/while
  153.1 4.0 %copy-start.4 = (f32[256,32]{0,1:T(8,128)}, f32[256,32]{0,1:T(8,128)S(1)}, u32[]{:S(2)}) copy-start(f32[256,32]{0,1:T(8,128)S(1)} %slice.1666) | copy-start | bytes 98308 | tf_op jit(solution)/shard_map/while
  153.2 2.4 copy-start.6
  153.3 1.6 copy-start.8
  154.0 0.7 slice-start.9
  158.6 0.7 slice-start.1
  169.5 11.2 %copy-start = (f32[256,128]{0,1:T(8,128)}, f32[256,128]{0,1:T(8,128)S(1)}, u32[]{:S(2)}) copy-start(f32[256,128]{0,1:T(8,128)S(1)} %slice.1658) | copy-start | bytes 393220 | tf_op jit(solution)/shard_map/while
  173.6 5.5 %copy-start.2 = (f32[256,64]{0,1:T(8,128)}, f32[256,64]{0,1:T(8,128)S(1)}, u32[]{:S(2)}) copy-start(f32[256,64]{0,1:T(8,128)S(1)} %slice.1665) | copy-start | bytes 196612 | tf_op jit(solution)/shard_map/while
  173.7 4.0 %copy-start.4 = (f32[256,32]{0,1:T(8,128)}, f32[256,32]{0,1:T(8,128)S(1)}, u32[]{:S(2)}) copy-start(f32[256,32]{0,1:T(8,128)S(1)} %slice.1666) | copy-start | bytes 98308 | tf_op jit(solution)/shard_map/while
  173.8 2.4 copy-start.6
  173.9 1.6 copy-start.8
  174.6 0.7 slice-start.9
  190.1 11.2 %copy-start = (f32[256,128]{0,1:T(8,128)}, f32[256,128]{0,1:T(8,128)S(1)}, u32[]{:S(2)}) copy-start(f32[256,128]{0,1:T(8,128)S(1)} %slice.1658) | copy-start | bytes 393220 | tf_op jit(solution)/shard_map/while
  194.3 5.5 %copy-start.2 = (f32[256,64]{0,1:T(8,128)}, f32[256,64]{0,1:T(8,128)S(1)}, u32[]{:S(2)}) copy-start(f32[256,64]{0,1:T(8,128)S(1)} %slice.1665) | copy-start | bytes 196612 | tf_op jit(solution)/shard_map/while
  194.4 4.0 %copy-start.4 = (f32[256,32]{0,1:T(8,128)}, f32[256,32]{0,1:T(8,128)S(1)}, u32[]{:S(2)}) copy-start(f32[256,32]{0,1:T(8,128)S(1)} %slice.1666) | copy-start | bytes 98308 | tf_op jit(solution)/shard_map/while
  194.5 2.4 copy-start.6
  194.5 1.6 copy-start.8
  (69 other events, 44.8 us)
Sparse Core Ops, SparseCore 0:
  259.4 48.3 all-reduce.134
where the time goes:
time: 318 us; the launch traced here: 316 us
  local copies, waits for them, and re-layouts  94.4 us (30%)
  waiting for transfers between devices  64.3 us (20%)
  other arithmetic  40.8 us (13%)
  between operations  37.4 us (12%)
  starting transfers between devices  36 us (11%)
  blocking collectives  23.2 us (7%)
  loops' own time  14 us (4%)
  matrix products  6.13 us (2%)
    psum x1, waiting for transfers between devices, per_device(): total = lax.psum(attr_grad, 'view')  48.5 us
    all_to_all x1, blocking collectives, per_device(): lax.all_to_all(grad_buffer.reshape(9, device_total, slot_capacity), 'dev'...  23.2 us
    all_to_all x1, starting transfers between devices, per_device(): lax.all_to_all(request.reshape(device_total, slot_capacity), 'dev', split...  19.5 us
    slice x180, local copies, waits for them, and re-layouts, tile_color(): keep = jnp.cumprod(1.0 - alpha, axis=1)  18.3 us
    all_to_all x1, starting transfers between devices, per_device(): lax.all_to_all(sent.reshape(9, device_total, slot_capacity), 'dev', split...  16.2 us
    all_to_all x1, waiting for transfers between devices, per_device(): lax.all_to_all(sent.reshape(9, device_total, slot_capacity), 'dev', split...  15.8 us
    split x48, local copies, waits for them, and re-layouts, tile_color(): keep = jnp.cumprod(1.0 - alpha, axis=1)  15.2 us
    another operation x1, loops' own time, composite(): color, grads = lax.map(tile_work, (rows_tiles, tile_ids, depth, cotangent))  14 us
  transfers between devices with their start and end apart: 3, of which 2 were waited for; matrix products, arithmetic and copies ran while one was open for 1% of the time, Pallas kernels for 0%

commit v1 on v0

--- a/solution.py
+++ b/solution.py
@@ -218,7 +218,7 @@
     ).reshape(9, -1)
     grad_rows = jnp.zeros((9, g_dev), jnp.float32).at[:, asked].add(returned)
     attr_grad = pull_owner(grad_rows)[0]
-    total = lax.psum(attr_grad, "view")
+    total = jnp.sum(lax.all_gather(attr_grad, "view"), axis=0)
     image = jnp.transpose(color, (1, 0, 2))[None]
     return (image, total)
 

time: 318 us -> 267 us (0.84)
  the two profiles are of different devices: /device:TPU:8 before, /device:TPU:32 now
where the time goes in v1:
time: 267 us; the launch traced here: 265 us
  local copies, waits for them, and re-layouts  92.3 us (35%)
  other arithmetic  39.9 us (15%)
  blocking collectives  36.7 us (14%)
  starting transfers between devices  35.4 us (13%)
  between operations  23.9 us (9%)
  waiting for transfers between devices  17.1 us (6%)
  loops' own time  14 us (5%)
  matrix products  6.13 us (2%)
    all_to_all x1, blocking collectives, per_device(): lax.all_to_all(grad_buffer.reshape(9, device_total, slot_capacity), 'dev'...  23.1 us
    all_to_all x1, starting transfers between devices, per_device(): lax.all_to_all(request.reshape(device_total, slot_capacity), 'dev', split...  19.2 us
    slice x180, local copies, waits for them, and re-layouts, tile_color(): keep = jnp.cumprod(1.0 - alpha, axis=1)  18.3 us
    all_to_all x1, waiting for transfers between devices, per_device(): lax.all_to_all(sent.reshape(9, device_total, slot_capacity), 'dev', split...  17.1 us
    all_to_all x1, starting transfers between devices, per_device(): lax.all_to_all(sent.reshape(9, device_total, slot_capacity), 'dev', split...  16.2 us
    split x48, local copies, waits for them, and re-layouts, tile_color(): keep = jnp.cumprod(1.0 - alpha, axis=1)  14.7 us
    another operation x1, loops' own time, composite(): color, grads = lax.map(tile_work, (rows_tiles, tile_ids, depth, cotangent))  14 us
    all_gather x1, blocking collectives, per_device(): total = jnp.sum(lax.all_gather(attr_grad, 'view'), axis=0)  13.6 us
  transfers between devices with their start and end apart: 2, of which 1 were waited for; matrix products, arithmetic and copies ran while one was open for 2% of the time, Pallas kernels for 0%

profile of v1, /device:TPU:32, one launch (start us, length us, event | category | flops | bytes accessed | tf_op | source)
XLA Modules:
  0.0 265.3 jit_solution(11223365229556573710)
XLA Ops:
  0.6 0.9 convert_reduce_fusion
  2.3 4.4 %sort.17 = (s32[1024]{0:T(1024)}, s32[1024]{0:T(1024)S(1)}) sort(s32[1024]{0:T(1024)S(1)} %bitcast.197, s32[1024]{0:T(1024)S(1)} %iota.41), dimensions={0}, to_apply=%region_1.0 | sort | flops 10240 | bytes 16384 | tf_op jit(solution)/shard_map/jit(argsort)/sort | solution.py:186
  7.4 4.5 %gather_fusion = s32[1024]{0:T(1024)S(1)} fusion(s32[1024]{0:T(1024)S(1)} %select_reduce_fusion, s32[1024]{0:T(1024)S(1)} %get-tuple-element.358), kind=kCustom, calls=%fused_computation | custom fusion | bytes 12288 | tf_op jit(solution)/shard_map/gather | solution.py:190
  12.0 4.3 %scatter_custom_fusion = s32[1024]{0:T(1024)S(1)} fusion(s32[1024]{0:T(1024)S(1)} %get-tuple-element.359, s32[1024]{0:T(1024)S(1)} %iota_subtract_fusion, s32[]{:T(128)} %constant.192.clone.1), kind=kCustom, calls=%fused_computation.292 | custom fusion | bytes 4100 | tf_op jit(solution)/shard_map/scatter | solution.py:190
  16.3 4.3 %scatter_custom_fusion.1 = s32[2048]{0:T(1024)S(1)} fusion(s32[1024]{0:T(1024)S(1)} %get-tuple-element.215, s32[1024]{0:T(1024)S(1)} %bitcast.204, s32[]{:T(128)} %constant.192.clone.1), kind=kCustom, calls=%fused_computation.165 | custom fusion | bytes 8196 | tf_op jit(solution)/shard_map/scatter | solution.py:193
  20.6 0.7 all_to_all.12
  21.3 19.2 %all-to-all-start = ((s32[128,1,16]{2,1,0:T(1,128)}), s32[128,1,16]{2,1,0:T(1,128)S(1)}, u32[]{:S(2)}, u32[]{:S(2)}) async-start(s32[128,1,16]{2,1,0:T(1,128)} %bitcast.48), calls=%async_computation | async-start | bytes 131072 | tf_op jit(solution)/shard_map/all_to_all | solution.py:194
  47.9 0.7 fusion.152
  67.5 2.0 fusion.143
  70.3 0.8 reduce.5
  71.2 5.5 %gather_fusion.1 = f32[2048,9]{1,0:T(8,128)S(1)} fusion(f32[9,512]{0,1:T(8,128)S(1)} %copy.57, s32[2048]{0:T(1024)S(1)} %broadcast_clamp_fusion), kind=kCustom, calls=%fused_computation.1 | custom fusion | bytes 155648 | tf_op jit(solution)/shard_map/gather | solution.py:203
  76.7 1.4 reshape.325
  78.2 16.2 %all-to-all-start.1 = ((f32[128,1,144]{2,1,0:T(1,128)}), f32[128,1,144]{2,1,0:T(1,128)S(1)}, u32[]{:S(2)}, u32[]{:S(2)}) async-start(f32[128,1,144]{2,1,0:T(1,128)} %reshape.325), calls=%async_computation.1 | async-start | bytes 262144 | tf_op jit(solution)/shard_map/all_to_all | solution.py:204
  94.5 17.1 %all-to-all-done.1 = f32[128,1,144]{2,1,0:T(1,128)S(1)} async-done(((f32[128,1,144]{2,1,0:T(1,128)}), f32[128,1,144]{2,1,0:T(1,128)S(1)}, u32[]{:S(2)}, u32[]{:S(2)}) %all-to-all-start.1) | async-done | bytes 73760 | tf_op jit(solution)/shard_map/all_to_all | solution.py:204
  112.1 1.0 reduce.6
  113.7 2.8 %gather_fusion.2 = f32[1024,9]{1,0:T(8,128)S(1)} fusion(f32[9,2048]{0,1:T(8,128)S(1)} %bitcast.148, s32[1024]{0:T(1024)S(1)} %get-tuple-element.214), kind=kCustom, calls=%fused_computation.2 | custom fusion | bytes 77824 | tf_op jit(solution)/shard_map/gather | solution.py:207
  117.4 81.8 %while.15 = (s32[]{:T(128)}, f32[4,3,256]{2,0,1:T(4,128)S(1)}, f32[4,9,256]{2,1,0:T(8,128)S(1)}, f32[4,9,256]{2,1,0:T(8,128)S(1)}, s32[4,256]{1,0:T(4,128)}, /*i...) while((s32[]{:T(128)}, f32[4,3,256]{2,0,1:T(4,128)S(1)}, ...), condition=%wide.region_14.15_spmd, body=%wide.region_7.14_spmd.sunk | while | flops 15078685 | bytes 22935272 | solution.py:166
  120.6 0.7 constant_dynamic-slice_fusion.10
  127.3 0.7 slice-done.9
  131.9 0.7 slice-done.1
  141.1 0.7 constant_dynamic-slice_fusion.10
  161.5 0.7 constant_dynamic-slice_fusion.10
  182.0 0.7 constant_dynamic-slice_fusion.10
  200.1 3.3 %scatter_custom_fusion.2 = f32[9,2048]{0,1:T(8,128)S(1)} fusion(s32[1024]{0:T(1024)S(1)} %get-tuple-element.215, f32[1024,9]{1,0:T(8,128)S(1)} %copy.62, f32[]{:T(128)} %constant.193.clone.1), kind=kCustom, calls=%fused_computation.138 | custom fusion | bytes 73732 | tf_op jit(solution)/shard_map/scatter | solution.py:210
  203.5 0.8 reshape.327
  204.2 23.1 %all_to_all.19 = f32[128,1,144]{2,1,0:T(1,128)S(1)} all-to-all(f32[128,1,144]{2,1,0:T(1,128)S(1)} %reshape.327), channel_id=1, replica_groups=mesh['view'=4,'dev'=128] {'dev'}, dimensions={0} | all-to-all | bytes 147456 | tf_op jit(solution)/shard_map/all_to_all | solution.py:212
  227.3 1.0 reduce.7
  228.9 11.5 %scatter_custom_fusion.3 = f32[9,512]{0,1:T(8,128)S(1)} fusion(s32[2048]{0:T(1024)S(1)} %bitcast.201, f32[2048,9]{1,0:T(8,128)S(1)} %bitcast.150, f32[]{:T(128)} %constant.193.clone.1), kind=kCustom, calls=%fused_computation.144 | custom fusion | flops 18432 | bytes 18436 | tf_op jit(solution)/shard_map/scatter-add | solution.py:219
  243.0 5.7 %fusion.98 = (f32[1,512]{1,0:T(1,128)S(1)}, f32[1,512]{1,0:T(1,128)S(1)}, f32[1,512]{1,0:T(1,128)S(1)}, f32[1,512]{1,0:T(1,128)S(1)}, f32[1,512]{1,0:T(1,128)S(1...) fusion(f32[1,512]{1,0:T(1,128)S(1)} %copy.82, f32[1,512]{1,0:T(1,128)S(1)} %copy.81, ...), kind=kLoop, calls=%fused_computation.325 | loop fusion | flops 81920 | bytes 100388 | tf_op jit(solution)/shard_map/transpose(jvp())/neg | solution.py:87
  248.7 1.9 negate_add_fusion.1
  251.1 13.6 %all-gather.1 = f32[4,59,512]{2,1,0:T(8,128)S(1)} all-gather(f32[1,59,512]{2,1,0:T(8,128)S(1)} %add_bitcast_fusion), channel_id=2, replica_groups=mesh['view'=4,'dev'=128] {'view'}, dimensions={0}, use_global_device_ids=true | all-gather | bytes 604160 | tf_op jit(solution)/shard_map/all_gather | solution.py:221
  264.7 0.7 reduce_sum.155
  (871 shorter events, 76.0 us)
Async XLA Ops:
  0.6 0.9 copy-start.16
  1.6 0.7 copy-start.12
  11.9 28.6 %copy-start.11 = (f32[59,512]{1,0:T(8,128)S(1)}, f32[59,512]{1,0:T(8,128)}, u32[]{:S(2)}) copy-start(f32[59,512]{1,0:T(8,128)} %param.8) | copy-start | bytes 362500
  21.3 48.5 %all-to-all-start = ((s32[128,1,16]{2,1,0:T(1,128)}), s32[128,1,16]{2,1,0:T(1,128)S(1)}, u32[]{:S(2)}, u32[]{:S(2)}) async-start(s32[128,1,16]{2,1,0:T(1,128)} %bitcast.48), calls=%async_computation | async-start | bytes 131072 | tf_op jit(solution)/shard_map/all_to_all | solution.py:194
  78.1 16.3 %copy-start.15 = (f32[1,3,4,256]{3,2,1,0:T(4,128)S(1)}, f32[1,3,4,256]{3,2,1,0:T(4,128)}, u32[]{:S(2)}) copy-start(f32[1,3,4,256]{3,2,1,0:T(4,128)} %param.13) | copy-start | bytes 36868
  78.2 33.4 %all-to-all-start.1 = ((f32[128,1,144]{2,1,0:T(1,128)}), f32[128,1,144]{2,1,0:T(1,128)S(1)}, u32[]{:S(2)}, u32[]{:S(2)}) async-start(f32[128,1,144]{2,1,0:T(1,128)} %reshape.325), calls=%async_computation.1 | async-start | bytes 262144 | tf_op jit(solution)/shard_map/all_to_all | solution.py:204
  122.2 11.1 %copy-start = (f32[256,128]{0,1:T(8,128)}, f32[256,128]{0,1:T(8,128)S(1)}, u32[]{:S(2)}) copy-start(f32[256,128]{0,1:T(8,128)S(1)} %slice.1658) | copy-start | bytes 393220 | tf_op jit(solution)/shard_map/while
  126.3 5.5 %copy-start.2 = (f32[256,64]{0,1:T(8,128)}, f32[256,64]{0,1:T(8,128)S(1)}, u32[]{:S(2)}) copy-start(f32[256,64]{0,1:T(8,128)S(1)} %slice.1665) | copy-start | bytes 196612 | tf_op jit(solution)/shard_map/while
  126.4 3.9 %copy-start.4 = (f32[256,32]{0,1:T(8,128)}, f32[256,32]{0,1:T(8,128)S(1)}, u32[]{:S(2)}) copy-start(f32[256,32]{0,1:T(8,128)S(1)} %slice.1666) | copy-start | bytes 98308 | tf_op jit(solution)/shard_map/while
  126.5 2.4 copy-start.6
  126.6 1.6 copy-start.8
  127.3 0.7 slice-start.9
  131.9 0.7 slice-start.1
  142.7 11.1 %copy-start = (f32[256,128]{0,1:T(8,128)}, f32[256,128]{0,1:T(8,128)S(1)}, u32[]{:S(2)}) copy-start(f32[256,128]{0,1:T(8,128)S(1)} %slice.1658) | copy-start | bytes 393220 | tf_op jit(solution)/shard_map/while
  146.8 5.5 %copy-start.2 = (f32[256,64]{0,1:T(8,128)}, f32[256,64]{0,1:T(8,128)S(1)}, u32[]{:S(2)}) copy-start(f32[256,64]{0,1:T(8,128)S(1)} %slice.1665) | copy-start | bytes 196612 | tf_op jit(solution)/shard_map/while
  146.9 3.9 %copy-start.4 = (f32[256,32]{0,1:T(8,128)}, f32[256,32]{0,1:T(8,128)S(1)}, u32[]{:S(2)}) copy-start(f32[256,32]{0,1:T(8,128)S(1)} %slice.1666) | copy-start | bytes 98308 | tf_op jit(solution)/shard_map/while
  147.0 2.4 copy-start.6
  147.1 1.6 copy-start.8
  147.8 0.7 slice-start.9
  152.3 0.7 slice-start.1
  163.2 11.1 %copy-start = (f32[256,128]{0,1:T(8,128)}, f32[256,128]{0,1:T(8,128)S(1)}, u32[]{:S(2)}) copy-start(f32[256,128]{0,1:T(8,128)S(1)} %slice.1658) | copy-start | bytes 393220 | tf_op jit(solution)/shard_map/while
  167.3 5.5 %copy-start.2 = (f32[256,64]{0,1:T(8,128)}, f32[256,64]{0,1:T(8,128)S(1)}, u32[]{:S(2)}) copy-start(f32[256,64]{0,1:T(8,128)S(1)} %slice.1665) | copy-start | bytes 196612 | tf_op jit(solution)/shard_map/while
  167.4 3.9 %copy-start.4 = (f32[256,32]{0,1:T(8,128)}, f32[256,32]{0,1:T(8,128)S(1)}, u32[]{:S(2)}) copy-start(f32[256,32]{0,1:T(8,128)S(1)} %slice.1666) | copy-start | bytes 98308 | tf_op jit(solution)/shard_map/while
  167.5 2.4 copy-start.6
  167.6 1.6 copy-start.8
  168.2 0.7 slice-start.9
  172.8 0.7 slice-start.1
  183.6 11.1 %copy-start = (f32[256,128]{0,1:T(8,128)}, f32[256,128]{0,1:T(8,128)S(1)}, u32[]{:S(2)}) copy-start(f32[256,128]{0,1:T(8,128)S(1)} %slice.1658) | copy-start | bytes 393220 | tf_op jit(solution)/shard_map/while
  187.7 5.5 %copy-start.2 = (f32[256,64]{0,1:T(8,128)}, f32[256,64]{0,1:T(8,128)S(1)}, u32[]{:S(2)}) copy-start(f32[256,64]{0,1:T(8,128)S(1)} %slice.1665) | copy-start | bytes 196612 | tf_op jit(solution)/shard_map/while
  187.8 3.9 %copy-start.4 = (f32[256,32]{0,1:T(8,128)}, f32[256,32]{0,1:T(8,128)S(1)}, u32[]{:S(2)}) copy-start(f32[256,32]{0,1:T(8,128)S(1)} %slice.1666) | copy-start | bytes 98308 | tf_op jit(solution)/shard_map/while
  187.9 2.4 copy-start.6
  188.0 1.6 copy-start.8
  (68 other events, 43.5 us)
